TPU v7x, 32 devices: a whole 2x2x4 slice. The times are simulated.
32 devices in a mesh: src: 32 (over z, y, x, core), dst: 1.
Axes of the slice: x: 2, y: 2, z: 4, core: 2. Of those that a mesh axis runs over, the one named last changes fastest.
Arguments:
- out_density: float32 [16384], P('src'), may hold values from 0.008 to 0.08
- in_density: float32 [16384], P('dst'), may hold values from 0.008 to 0.08
- retention: float32 [16384], P('src'), may hold values from 0.15 to 0.75
- demand: float32 [16384], P('src'), may hold values from 0.5 to 4
- location: int32 [16384], replicated, may hold values from 0 to 16383
- scenario_blocks: int32 [32], replicated, may hold values from 0 to 127
Outputs:
- out_fitness: float32 [16384], P('src')
- in_fitness: float32 [16384], P('dst')
- levels: float32 [16384, 32], P('src', 'dst')
Inputs may be any that keep to these rules, and one draw needn't show every extreme that they name: `scenario_blocks`: scenario k extracts the 128 firms of block index b = scenario_blocks_k, firms 128 * b to 128 * b + 127. `location`: several firms may share a map cell, and some cells hold none.
All inputs are finite; a program needn't handle non-finite values.
Results may differ from a plain program's by a relative error of at most 0.0003.
Values sent between devices are 32-bit elements; how exact they have to be, the bound alone decides.
A program may use at most 64 MiB of HBM per device.

v0:
```python
import math

import jax
import jax.numpy as jnp
from jax import lax
from jax.sharding import PartitionSpec as P

SWEEPS = 2
ITERS = 2
EXTRACT = 128
MAP_SIDE = 256
RANGE = 18


far_weight = 0.015625


def on_device(out_density, in_density, retention, demand, location, scenario_blocks):
    rows_dev = out_density.shape[0]
    cols_dev = in_density.shape[0]
    firms = rows_dev * lax.axis_size("src")
    row_start = lax.axis_index("src") * rows_dev
    col_start = lax.axis_index("dst") * cols_dev
    height = math.gcd(rows_dev, 128)
    blocks = rows_dev // height
    col_ids = col_start + jnp.arange(cols_dev, dtype=jnp.int32)
    offsets = jnp.arange(blocks, dtype=jnp.int32) * height
    src_cells = lax.dynamic_slice_in_dim(location, row_start, rows_dev)
    dst_cells = lax.dynamic_slice_in_dim(location, col_start, cols_dev)
    src_row = src_cells // MAP_SIDE
    src_col = src_cells % MAP_SIDE
    dst_row = dst_cells // MAP_SIDE
    dst_col = dst_cells % MAP_SIDE
    out_fit = jnp.sqrt(out_density)
    in_fit = jnp.sqrt(in_density)

    def pair_weight(offset):
        row_ids = row_start + offset + jnp.arange(height, dtype=jnp.int32)
        row_gap = lax.dynamic_slice_in_dim(src_row, offset, height)[:, None] - dst_row[None, :]
        col_gap = lax.dynamic_slice_in_dim(src_col, offset, height)[:, None] - dst_col[None, :]
        nearby = row_gap * row_gap + col_gap * col_gap <= RANGE * RANGE
        affinity = jnp.where(nearby, 1.0, far_weight)
        return jnp.where(row_ids[:, None] != col_ids[None, :], affinity, 0.0)

    for sweep_no in range(SWEEPS):

        def row_part(offset):
            row_fit = lax.dynamic_slice_in_dim(out_fit, offset, height)
            weight = pair_weight(offset)
            ratios = weight * in_fit[None, :] / (1.0 + row_fit[:, None] * in_fit[None, :] * weight)
            return jnp.sum(ratios, axis=1)

        row_partial = lax.map(row_part, offsets).reshape(rows_dev)
        row_total = lax.psum(row_partial, "dst")
        out_fit = firms * out_density / row_total

        def col_part(running, offset):
            row_fit = lax.dynamic_slice_in_dim(out_fit, offset, height)
            weight = pair_weight(offset)
            ratios = weight * row_fit[:, None] / (1.0 + row_fit[:, None] * in_fit[None, :] * weight)
            return (running + jnp.sum(ratios, axis=0), None)

        col_partial, _ = lax.scan(col_part, jnp.zeros((cols_dev,), jnp.float32), offsets)
        col_total = lax.psum(col_partial, "src")
        in_fit = firms * in_density / col_total
    row_scale = retention / (firms * out_density)

    def coeff_block(offset):
        row_fit = lax.dynamic_slice_in_dim(out_fit, offset, height)
        scale_part = lax.dynamic_slice_in_dim(row_scale, offset, height)
        product = row_fit[:, None] * in_fit[None, :] * pair_weight(offset)
        chance = product / (1.0 + product)
        return chance * scale_part[:, None]

    coefficients = lax.map(coeff_block, offsets).reshape(rows_dev, cols_dev)
    scenarios = scenario_blocks.shape[0]
    portion = scenarios // lax.axis_size("dst")
    leading = lax.axis_index("dst") * portion
    firm_rows = row_start + jnp.arange(rows_dev, dtype=jnp.int32)
    retained = (firm_rows[:, None] // EXTRACT != scenario_blocks[None, :]).astype(jnp.float32)
    levels = retained * demand[:, None]
    for round_no in range(ITERS):
        every_row = lax.all_gather(levels, "src", axis=0, tiled=True)
        columns = lax.dynamic_slice_in_dim(every_row, col_start, cols_dev, 0)
        summed = lax.psum(
            jnp.dot(
                coefficients,
                columns,
                preferred_element_type=jnp.float32,
                precision=lax.Precision.HIGHEST,
            ),
            "dst",
        )
        levels = retained * (demand[:, None] + summed)
    result = lax.dynamic_slice_in_dim(levels, leading, portion, 1)
    return (out_fit, in_fit, result)


def solution(mesh):
    in_specs = (P("src"), P("dst"), P("src"), P("src"), P(), P())
    out_specs = (P("src"), P("dst"), P("src", "dst"))
    return jax.shard_map(
        on_device, mesh=mesh, in_specs=in_specs, out_specs=out_specs, check_vma=False
    )
```

profile of v0, /device:TPU:0, one launch (start us, length us, event | category | flops | bytes accessed | tf_op | source)
XLA Modules:
  0.0 580.2 jit_solution(1393125838560426272)
XLA Ops:
  7.3 0.9 add_select_fusion
  8.2 0.8 add_select_fusion.3
  8.9 0.9 sqrt.6
  9.8 0.7 sqrt.7
  10.5 33.4 %while.55 = (s32[]{:T(128)}, f32[4,128]{1,0:T(4,128)S(1)}, s32[4]{0:T(128)S(1)}, s32[]{:T(128)}, s32[512]{0:T(512)S(1)}, /*index=5*/s32[16384]{0:T(1024)S(1)}, s...) while((s32[]{:T(128)}, f32[4,128]{1,0:T(4,128)S(1)}, ...), condition=%wide.region_2.3_spmd.clone, body=%wide.region_0.2_spmd.clone.sunk | while | flops 31457284 | bytes 203979 | solution.py:53
  10.5 0.6 dynamic_slice.120
  13.9 4.9 fusion.33
  18.9 0.6 dynamic_slice.120
  22.3 4.9 fusion.33
  27.2 0.6 dynamic_slice.120
  30.6 4.9 fusion.33
  39.0 4.9 fusion.33
  43.9 0.7 bitcast_divide_fusion.1
  44.6 34.3 %while.58 = (s32[]{:T(128)}, f32[16384]{0:T(1024)S(1)}, s32[4]{0:T(128)S(1)}, s32[]{:T(128)}, s32[512]{0:T(512)S(1)}, /*index=5*/s32[16384]{0:T(1024)S(1)}, s32[...) while((s32[]{:T(128)}, f32[16384]{0:T(1024)S(1)}, ...), condition=%wide.region_5.6_spmd.clone, body=%wide.region_3.5_spmd.clone.sunk | while | flops 31473796 | bytes 464593 | solution.py:63
  44.6 0.6 dynamic_slice.133
  48.0 5.1 fusion.36
  53.2 0.6 dynamic_slice.133
  56.6 5.1 fusion.36
  61.8 0.6 dynamic_slice.133
  65.2 5.1 fusion.36
  73.8 5.1 fusion.36
  79.0 0.6 copy-done.1
  79.7 120.3 %all-reduce.3.cloned.1.call-done = f32[16384]{0:T(1024)} async-done(((f32[16384]{0:T(1024)}), f32[16384]{0:T(1024)}) %all-reduce.3.cloned.1.call-update) | async-done | bytes 65552 | tf_op jit(solution)/shard_map/psum | solution.py:64
  200.0 0.9 multiply_divide_fusion.1
  200.9 33.4 %while.56 = (s32[]{:T(128)}, f32[4,128]{1,0:T(4,128)S(1)}, s32[4]{0:T(128)S(1)}, s32[]{:T(128)}, s32[512]{0:T(512)S(1)}, /*index=5*/s32[16384]{0:T(1024)S(1)}, s...) while((s32[]{:T(128)}, f32[4,128]{1,0:T(4,128)S(1)}, ...), condition=%wide.region_9.10_spmd.clone, body=%wide.region_7.9_spmd.clone.sunk | while | flops 31457284 | bytes 203979 | solution.py:53
  204.3 4.9 fusion.34
  212.7 4.9 fusion.34
  221.0 4.9 fusion.34
  229.4 4.9 fusion.34
  234.3 0.7 multiply_divide_fusion.2
  235.0 34.3 %while.59 = (s32[]{:T(128)}, f32[16384]{0:T(1024)S(1)}, s32[4]{0:T(128)S(1)}, s32[]{:T(128)}, s32[512]{0:T(512)S(1)}, /*index=5*/s32[16384]{0:T(1024)S(1)}, s32[...) while((s32[]{:T(128)}, f32[16384]{0:T(1024)S(1)}, ...), condition=%wide.region_12.13_spmd.clone, body=%wide.region_10.12_spmd.clone.sunk | while | flops 31473796 | bytes 464593 | solution.py:63
  238.4 5.1 fusion.37
  247.0 5.1 fusion.37
  255.6 5.1 fusion.37
  264.2 5.1 fusion.37
  269.4 0.6 copy-done.2
  270.1 0.7 compare_select_fusion
  271.0 117.5 %all-reduce.5.cloned.1.call-done = f32[16384]{0:T(1024)} async-done(((f32[16384]{0:T(1024)}), f32[16384]{0:T(1024)}) %all-reduce.5.cloned.1.call-update) | async-done | bytes 65552 | tf_op jit(solution)/shard_map/psum | solution.py:64
  388.5 0.9 multiply_divide_fusion
  389.4 39.0 %while.57 = (s32[]{:T(128)}, f32[4,128,16384]{2,1,0:T(8,128)}, s32[4]{0:T(128)S(1)}, f32[512]{0:T(512)S(1)}, f32[16384]{0:T(1024)S(1)}, /*index=5*/s32[]{:T(128)...) while((s32[]{:T(128)}, f32[4,128,16384]{2,1,0:T(8,128)}, ...), condition=%wide.region_15.16_spmd.clone, body=%wide.region_14.15_spmd.clone.sunk | while | flops 29360260 | bytes 8593107 | solution.py:75
  392.9 6.3 %fusion.35 = f32[4,128,16384]{2,1,0:T(8,128)} fusion(f32[4,128,16384]{2,1,0:T(8,128)} %get-tuple-element.1026, s32[]{:T(128)} %get-tuple-element.1025, f32[128]{0:T(128)S(1)} %dynamic_slice.129, s32[16384]{0:T(1024)S(1)} %get-tuple-element.1048, s32[128]{0:T(128)S(1)} %dynamic_slice.130, s32[16384]{0:T(1024)S(1)} %get-tuple-element.1046, ...), kind=kLoop, calls=%fused_computation.17.clone.1 | loop fusion | flops 29360128 | bytes 8588288 | tf_op jit(solution)/shard_map/while/body/jit(dynamic_update_index_in_dim)/dynamic_update_slice | solution.py:75
  402.6 6.2 %fusion.35 = f32[4,128,16384]{2,1,0:T(8,128)} fusion(f32[4,128,16384]{2,1,0:T(8,128)} %get-tuple-element.1026, s32[]{:T(128)} %get-tuple-element.1025, f32[128]{0:T(128)S(1)} %dynamic_slice.129, s32[16384]{0:T(1024)S(1)} %get-tuple-element.1048, s32[128]{0:T(128)S(1)} %dynamic_slice.130, s32[16384]{0:T(1024)S(1)} %get-tuple-element.1046, ...), kind=kLoop, calls=%fused_computation.17.clone.1 | loop fusion | flops 29360128 | bytes 8588288 | tf_op jit(solution)/shard_map/while/body/jit(dynamic_update_index_in_dim)/dynamic_update_slice | solution.py:75
  412.4 6.3 %fusion.35 = f32[4,128,16384]{2,1,0:T(8,128)} fusion(f32[4,128,16384]{2,1,0:T(8,128)} %get-tuple-element.1026, s32[]{:T(128)} %get-tuple-element.1025, f32[128]{0:T(128)S(1)} %dynamic_slice.129, s32[16384]{0:T(1024)S(1)} %get-tuple-element.1048, s32[128]{0:T(128)S(1)} %dynamic_slice.130, s32[16384]{0:T(1024)S(1)} %get-tuple-element.1046, ...), kind=kLoop, calls=%fused_computation.17.clone.1 | loop fusion | flops 29360128 | bytes 8588288 | tf_op jit(solution)/shard_map/while/body/jit(dynamic_update_index_in_dim)/dynamic_update_slice | solution.py:75
  422.1 6.2 %fusion.35 = f32[4,128,16384]{2,1,0:T(8,128)} fusion(f32[4,128,16384]{2,1,0:T(8,128)} %get-tuple-element.1026, s32[]{:T(128)} %get-tuple-element.1025, f32[128]{0:T(128)S(1)} %dynamic_slice.129, s32[16384]{0:T(1024)S(1)} %get-tuple-element.1048, s32[128]{0:T(128)S(1)} %dynamic_slice.130, s32[16384]{0:T(1024)S(1)} %get-tuple-element.1046, ...), kind=kLoop, calls=%fused_computation.17.clone.1 | loop fusion | flops 29360128 | bytes 8588288 | tf_op jit(solution)/shard_map/while/body/jit(dynamic_update_index_in_dim)/dynamic_update_slice | solution.py:75
  428.3 20.0 %all-gather.3.cloned.1.call-done = f32[16384,32]{0,1:T(8,128)} async-done(((f32[512,32]{0,1:T(8,128)}), f32[16384,32]{0,1:T(8,128)}) %all-gather.3.cloned.1.call-update) | async-done | bytes 2097168 | tf_op jit(solution)/shard_map/all_gather | solution.py:83
  448.4 35.0 %fusion.17 = f32[512,32]{0,1:T(8,128)} fusion(f32[512,16384]{1,0:T(8,128)} %bitcast.30, f32[16384,32]{0,1:T(8,128)} %all-gather.3.cloned.1.call-done, f32[512]{0:T(512)S(1)} %copy-done.4, s32[512]{0:T(512)S(1)} %add_select_fusion.2, s32[32]{0:T(128)S(1)} %copy-done.5), kind=kOutput, calls=%fused_computation.36 | convolution fusion | flops 3221274624 | bytes 35721344 | tf_op jit(solution)/shard_map/dot_general | solution.py:86
  483.4 55.3 %all-gather.5.cloned.1.call-done = f32[16384,32]{0,1:T(8,128)} async-done(((f32[512,32]{0,1:T(8,128)}), f32[16384,32]{0,1:T(8,128)}) %all-gather.5.cloned.1.call-update) | async-done | bytes 2097168 | tf_op jit(solution)/shard_map/all_gather | solution.py:83
  538.7 35.0 %fusion.16 = f32[512,32]{0,1:T(8,128)} fusion(f32[512,16384]{1,0:T(8,128)} %bitcast.31, f32[16384,32]{0,1:T(8,128)} %all-gather.5.cloned.1.call-done, f32[512]{0:T(512)S(1)} %copy-done.4, s32[512]{0:T(512)S(1)} %add_select_fusion.2, s32[32]{0:T(128)S(1)} %copy-done.5), kind=kOutput, calls=%fused_computation.34 | convolution fusion | flops 3221274624 | bytes 35721344 | tf_op jit(solution)/shard_map/dot_general | solution.py:86
  (141 shorter events, 14.0 us)
Async XLA Ops:
  7.2 381.3 %copy-start.3 = (f32[16384]{0:T(1024)S(1)}, f32[16384]{0:T(1024)}, u32[]{:S(2)}) copy-start(f32[16384]{0:T(1024)} %param.17) | copy-start | bytes 196612
  7.2 262.9 %copy-start.4 = (f32[512]{0:T(512)S(1)}, f32[512]{0:T(512)}, u32[]{:S(2)}) copy-start(f32[512]{0:T(512)} %param.19) | copy-start | bytes 6148
  7.2 262.9 %copy-start.5 = (s32[32]{0:T(128)S(1)}, s32[32]{0:T(128)}, u32[]{:S(2)}) copy-start(s32[32]{0:T(128)} %param.21) | copy-start | bytes 388
  7.2 192.8 %all-reduce.3.cloned.1.call-start = ((), (), s32[]{:S(2)}) async-start(), calls=%async_computation | async-start | bytes 131072 | tf_op jit(solution)/shard_map/psum | solution.py:64
  78.9 0.6 copy-start.1
  79.6 308.9 %all-reduce.5.cloned.1.call-start = ((), (), s32[]{:S(2)}) async-start(), calls=%async_computation.1 | async-start | bytes 131072 | tf_op jit(solution)/shard_map/psum | solution.py:64
  269.4 0.6 copy-start.2
  270.0 178.4 %all-gather.3.cloned.1.call-start = ((), (), s32[]{:S(2)}) async-start(), calls=%async_computation.2 | async-start | bytes 2162688 | tf_op jit(solution)/shard_map/all_gather | solution.py:83
  270.8 267.9 %all-gather.5.cloned.1.call-start = ((), (), s32[]{:S(2)}) async-start(), calls=%async_computation.3 | async-start | bytes 2162688 | tf_op jit(solution)/shard_map/all_gather | solution.py:83
  428.3 55.1 %copy-start = (f32[16384]{0:T(1024)}, f32[16384]{0:T(1024)S(1)}, u32[]{:S(2)}) copy-start(f32[16384]{0:T(1024)S(1)} %get-tuple-element.1067) | copy-start | bytes 196612
  428.3 55.1 %copy-start.6 = (f32[512]{0:T(512)}, f32[512]{0:T(512)S(1)}, u32[]{:S(2)}) copy-start(f32[512]{0:T(512)S(1)} %get-tuple-element.1081) | copy-start | bytes 6148
Sparse Core Ops, SparseCore 0:
  79.7 120.2 all-reduce.2
  270.1 118.3 all-reduce.4
  391.4 56.9 all-gather.2
  483.5 55.1 all-gather.4
where the time goes:
time: 581 us; the launch traced here: 580 us
  waiting for transfers between devices  313 us (54%)
  other arithmetic  111 us (19%)
  matrix products  70 us (12%)
  loops' own time  52.4 us (9%)
  local copies, waits for them, and re-layouts  19.6 us (3%)
  between operations  13.9 us (2%)
    psum x2, waiting for transfers between devices, on_device(): col_total = lax.psum(col_partial, 'src')  238 us
    all_gather x2, waiting for transfers between devices, on_device(): every_row = lax.all_gather(levels, 'src', axis=0, tiled=True)  75.3 us
    dot_general x2, matrix products, on_device(): jnp.dot(coefficients, columns, preferred_element_type=jnp.float32, precis...  70 us
    reduce_sum x8, other arithmetic, col_part(): return (running + jnp.sum(ratios, axis=0), None)  40.9 us
    reduce_sum x8, other arithmetic, row_part(): return jnp.sum(ratios, axis=1)  39.1 us
    dynamic_update_slice x4, other arithmetic, on_device(): coefficients = lax.map(coeff_block, offsets).reshape(rows_dev, cols_dev)  25 us
    another operation x2, loops' own time, on_device(): lax.scan(col_part, jnp.zeros((cols_dev,), jnp.float32), offsets)  21.1 us
    another operation x2, loops' own time, on_device(): row_partial = lax.map(row_part, offsets).reshape(rows_dev)  20.9 us
  transfers between devices with their start and end apart: 4, of which 4 were waited for; matrix products, arithmetic and copies ran while one was open for 5% of the time, Pallas kernels for 0%

commit v1 on v0

--- a/solution.py
+++ b/solution.py
@@ -1,8 +1,11 @@
+import functools
 import math
 
 import jax
 import jax.numpy as jnp
 from jax import lax
+from jax.experimental import pallas as pl
+from jax.experimental.pallas import tpu as pltpu
 from jax.sharding import PartitionSpec as P
 
 SWEEPS = 2
@@ -13,6 +16,298 @@
 
 
 far_weight = 0.015625
+FAR = 64.0
+ROWS = 64
+LANES = 128
+
+
+def kernel(
+    n,
+    left_ref,
+    right_ref,
+    od_ref,
+    ret_ref,
+    dem_ref,
+    dem_row_ref,
+    ind_ref,
+    scen_ref,
+    x_out,
+    y_out,
+    lev_out,
+    bmat,
+    hi_ref,
+    lo_ref,
+    rowacc,
+    xb,
+    vb,
+    part,
+    gath,
+    yrow,
+    urow,
+    dem_all,
+    lev_all,
+    acc,
+    send_sem,
+    one_sem,
+    lev_sem,
+):
+    me = lax.axis_index("src")
+    rows, cols = bmat.shape
+    firms = rows * n
+    scen = scen_ref.shape[0]
+    wide = rows // LANES
+
+    barrier = pltpu.get_barrier_semaphore()
+
+    @pl.loop(1, n)
+    def _(s):
+        pl.semaphore_signal(barrier, inc=1, device_id={"src": lax.rem(me + s, n)})
+
+    pl.semaphore_wait(barrier, n - 1)
+
+    def push(src, dst, sems, phase):
+        @pl.loop(1, n)
+        def _(s):
+            q = lax.rem(me + n - s, n)
+            pltpu.make_async_remote_copy(
+                src_ref=src(q),
+                dst_ref=dst.at[me],
+                send_sem=send_sem.at[phase],
+                recv_sem=sems,
+                device_id={"src": q},
+            ).start()
+
+    def drain(buf, sem):
+        some = buf.at[pl.ds(0, n - 1)]
+        pltpu.make_async_copy(some, some, sem).wait()
+
+    dem_all[me] = dem_row_ref[...]
+    push(lambda q: dem_row_ref, dem_all, one_sem.at[0], 0)
+
+    @pl.loop(0, n)
+    def _(q):
+        c0 = pl.multiple_of(q * rows, rows)
+        dist = jnp.dot(
+            left_ref[...],
+            right_ref[:, pl.ds(c0, rows)],
+            preferred_element_type=jnp.float32,
+        )
+        bmat[:, pl.ds(c0, rows)] = jnp.where(dist <= RANGE * RANGE, 1.0, FAR)
+
+    mine = pl.ds(pl.multiple_of(me * rows, rows), rows)
+    for r0 in range(0, rows, ROWS):
+        shape = (ROWS, rows)
+        same = lax.broadcasted_iota(jnp.int32, shape, 0) + r0 == lax.broadcasted_iota(
+            jnp.int32, shape, 1
+        )
+        bmat[pl.ds(r0, ROWS), mine] = jnp.where(same, jnp.inf, bmat[pl.ds(r0, ROWS), mine])
+
+    xb[...] = jnp.broadcast_to(jnp.sqrt(od_ref[...]), xb.shape)
+
+    @pl.loop(0, n)
+    def _(q):
+        c0 = pl.multiple_of(q * rows, rows)
+        y = jnp.sqrt(ind_ref[q])
+        yrow[:, pl.ds(c0, rows)] = y
+        urow[:, pl.ds(c0, rows)] = 1.0 / y
+
+    tiles = 16
+    strip = tiles * LANES
+    for sweep in range(SWEEPS):
+        @pl.loop(0, rows // ROWS)
+        def _(b):
+            rs = pl.ds(pl.multiple_of(b * ROWS, ROWS), ROWS)
+            x = xb[rs, :]
+
+            def body(c, total):
+                c0 = pl.multiple_of(c * strip, strip)
+                for t in range(tiles):
+                    cs = pl.ds(c0 + t * LANES, LANES)
+                    total = total + pl.reciprocal(bmat[rs, cs] * urow[:, cs] + x, approx=True)
+                return total
+
+            rowacc[rs, :] = lax.fori_loop(
+                0, cols // strip, body, jnp.zeros((ROWS, LANES), jnp.float32)
+            )
+
+        row_total = jnp.sum(rowacc[...], axis=1, keepdims=True)
+        x_new = firms * od_ref[...] / row_total
+        xb[...] = jnp.broadcast_to(x_new, xb.shape)
+        vb[...] = jnp.broadcast_to(1.0 / x_new, vb.shape)
+
+        @pl.loop(0, n)
+        def _(q):
+            c0 = pl.multiple_of(q * rows, rows)
+            for t in range(wide):
+                cs = pl.ds(c0 + t * LANES, LANES)
+                y = yrow[:, cs]
+                total = jnp.zeros((8, LANES), jnp.float32)
+                for r0 in range(0, rows, ROWS):
+                    rs = pl.ds(r0, ROWS)
+                    term = pl.reciprocal(bmat[rs, cs] * vb[rs, :] + y, approx=True)
+                    total = total + jnp.sum(term.reshape(ROWS // 8, 8, LANES), axis=0)
+                part[sweep, q, :, pl.ds(t * LANES, LANES)] = jnp.sum(total, axis=0, keepdims=True)
+
+        gath[2 * sweep, me] = part[sweep, me]
+        push(lambda q: part.at[sweep, q], gath.at[2 * sweep], one_sem.at[1 + 2 * sweep], 1 + 2 * sweep)
+        drain(gath.at[2 * sweep], one_sem.at[1 + 2 * sweep])
+        col_total = jnp.sum(gath[2 * sweep], axis=0)
+        fresh = gath.at[2 * sweep + 1]
+        fresh[me] = firms * ind_ref[me] / col_total
+        push(lambda q: fresh.at[me], fresh, one_sem.at[2 + 2 * sweep], 2 + 2 * sweep)
+        drain(fresh, one_sem.at[2 + 2 * sweep])
+
+        @pl.loop(0, n)
+        def _(q):
+            c0 = pl.multiple_of(q * rows, rows)
+            y = fresh[q]
+            yrow[:, pl.ds(c0, rows)] = y
+            urow[:, pl.ds(c0, rows)] = 1.0 / y
+
+    y_out[...] = gath[2 * SWEEPS - 1]
+    x_new = xb[:, 0:1]
+    x_out[...] = x_new
+    gain = x_new * (ret_ref[...] / (firms * od_ref[...]))
+    drain(dem_all, one_sem.at[0])
+
+    def kept(q):
+        ids = q * rows + lax.broadcasted_iota(jnp.int32, (scen, rows), 1)
+        return lax.div(ids, EXTRACT) != scen_ref[...]
+
+    def product(levels):
+        top = levels.astype(jnp.bfloat16)
+        low = (levels - top.astype(jnp.float32)).astype(jnp.bfloat16)
+        both = jnp.concatenate([top, low], axis=0)
+        dims = (((1,), (1,)), ((), ()))
+        acc[...] += lax.dot_general(
+            hi_ref[...], both, dims, preferred_element_type=jnp.float32
+        ) + lax.dot_general(lo_ref[...], both, dims, preferred_element_type=jnp.float32)
+
+    def split(rs, value):
+        top = value.astype(jnp.bfloat16)
+        hi_ref[rs, :] = top
+        lo_ref[rs, :] = (value - top.astype(jnp.float32)).astype(jnp.bfloat16)
+
+    acc[...] = jnp.zeros_like(acc)
+
+    @pl.loop(0, n)
+    def _(q):
+        cs = pl.ds(pl.multiple_of(q * rows, rows), rows)
+        u = urow[:, cs]
+        for r0 in range(0, rows, ROWS):
+            rs = pl.ds(r0, ROWS)
+            x = jnp.concatenate([xb[rs, :]] * wide, axis=1)
+            value = pl.reciprocal(bmat[rs, cs] * u + x, approx=True)
+            bmat[rs, cs] = value
+            split(rs, value)
+        product(jnp.where(kept(q), dem_all[q], 0.0))
+
+    summed = gain * (acc[:, 0:scen] + acc[:, scen:])
+    keep_mine = kept(me)
+    fresh_levels = jnp.where(keep_mine, dem_row_ref[...] + summed.T, 0.0)
+    lev_all[me] = fresh_levels
+    acc[...] = jnp.zeros_like(acc)
+    lev_mine = lev_all.at[me]
+
+    @pl.loop(1, n)
+    def _(s):
+        q = lax.rem(me + n - s, n)
+        pltpu.make_async_remote_copy(
+            src_ref=lev_mine,
+            dst_ref=lev_all.at[me],
+            send_sem=send_sem.at[5],
+            recv_sem=lev_sem.at[me],
+            device_id={"src": q},
+        ).start()
+
+    @pl.loop(0, n)
+    def _(s):
+        q = lax.rem(me + s, n)
+        cs = pl.ds(pl.multiple_of(q * rows, rows), rows)
+        for r0 in range(0, rows, ROWS):
+            rs = pl.ds(r0, ROWS)
+            split(rs, bmat[rs, cs])
+
+        @pl.when(s > 0)
+        def _():
+            slot = lev_all.at[q]
+            pltpu.make_async_copy(slot, slot, lev_sem.at[q]).wait()
+
+        product(lev_all[q])
+
+    summed = gain * (acc[:, 0:scen] + acc[:, scen:])
+    ids = me * rows + lax.broadcasted_iota(jnp.int32, (scen, rows), 1)
+    lev_out[...] = jnp.where(keep_mine, dem_row_ref[...] + summed.T, 0.0).T
+
+    drain(dem_all, send_sem.at[0])
+    for phase in range(1, 5):
+        drain(gath.at[0], send_sem.at[phase])
+    drain(lev_all, send_sem.at[5])
+
+
+def fused(out_density, in_density, retention, demand, location, scenario_blocks):
+    rows = out_density.shape[0]
+    cols = in_density.shape[0]
+    n = lax.axis_size("src")
+    scen = scenario_blocks.shape[0]
+    mine = lax.dynamic_slice_in_dim(location, lax.axis_index("src") * rows, rows)
+
+    def bytes_of(norm):
+        return norm >> 16, (norm >> 8) & 255, norm & 255
+
+    def features(cells, left):
+        r, c = cells // MAP_SIDE, cells % MAP_SIDE
+        norm = bytes_of(r * r + c * c)
+        one = jnp.ones_like(r)
+        scale = (65536 * one, 256 * one, one)
+        head = (-2 * r, -2 * c) if left else (r, c)
+        tail = norm + scale if left else scale + norm
+        zero = jnp.zeros_like(r)
+        return jnp.stack(head + tail + (zero,) * 8, axis=1 if left else 0).astype(jnp.bfloat16)
+
+    vmem = pl.BlockSpec(memory_space=pltpu.VMEM)
+    f32 = jnp.float32
+    x, y, levels = pl.pallas_call(
+        functools.partial(kernel, n),
+        out_shape=(
+            jax.ShapeDtypeStruct((rows, 1), f32),
+            jax.ShapeDtypeStruct((n, 1, rows), f32),
+            jax.ShapeDtypeStruct((rows, scen), f32),
+        ),
+        in_specs=[vmem] * 8,
+        out_specs=(vmem,) * 3,
+        scratch_shapes=[
+            pltpu.VMEM((rows, cols), f32),
+            pltpu.VMEM((rows, rows), jnp.bfloat16),
+            pltpu.VMEM((rows, rows), jnp.bfloat16),
+            pltpu.VMEM((rows, LANES), f32),
+            pltpu.VMEM((rows, LANES), f32),
+            pltpu.VMEM((rows, LANES), f32),
+            pltpu.VMEM((SWEEPS, n, 1, rows), f32),
+            pltpu.VMEM((2 * SWEEPS, n, 1, rows), f32),
+            pltpu.VMEM((1, cols), f32),
+            pltpu.VMEM((1, cols), f32),
+            pltpu.VMEM((n, 1, rows), f32),
+            pltpu.VMEM((n, scen, rows), f32),
+            pltpu.VMEM((rows, 2 * scen), f32),
+            pltpu.SemaphoreType.DMA((6,)),
+            pltpu.SemaphoreType.DMA((5,)),
+            pltpu.SemaphoreType.DMA((n,)),
+        ],
+        compiler_params=pltpu.CompilerParams(
+            collective_id=0, has_side_effects=True, vmem_limit_bytes=56 * 2**20
+        ),
+    )(
+        features(mine, True),
+        features(location, False),
+        out_density[:, None],
+        retention[:, None],
+        demand[:, None],
+        demand[None, :],
+        in_density.reshape(n, 1, rows),
+        scenario_blocks[:, None],
+    )
+    return x.reshape(rows), y.reshape(cols), levels
 
 
 def on_device(out_density, in_density, retention, demand, location, scenario_blocks):
@@ -96,9 +391,19 @@
     return (out_fit, in_fit, result)
 
 
+def program(out_density, in_density, retention, demand, location, scenario_blocks):
+    args = (out_density, in_density, retention, demand, location, scenario_blocks)
+    rows = out_density.shape[0]
+    cols = in_density.shape[0]
+    whole = lax.axis_size("dst") == 1
+    if whole and rows % (2 * LANES) == 0 and cols % (16 * LANES) == 0:
+        return fused(*args)
+    return on_device(*args)
+
+
 def solution(mesh):
     in_specs = (P("src"), P("dst"), P("src"), P("src"), P(), P())
     out_specs = (P("src"), P("dst"), P("src", "dst"))
     return jax.shard_map(
-        on_device, mesh=mesh, in_specs=in_specs, out_specs=out_specs, check_vma=False
+        program, mesh=mesh, in_specs=in_specs, out_specs=out_specs, check_vma=False
     )

time: 581 us -> 152 us (0.26)
  waiting for transfers between devices: 313 us -> 0 us
  Pallas kernels: 0 us -> 139 us
  other arithmetic: 111 us -> 1.61 us
  matrix products: 70 us -> 0 us
  loops' own time: 52.4 us -> 0 us
  between operations: 13.9 us -> 0.82 us
  local copies, waits for them, and re-layouts: 19.6 us -> 9.85 us
    psum x2 -> x0, waiting for transfers between devices: 238 us -> none  [on_device(): col_total = lax.psum(col_partial, 'src')]
    pallas_call x0 -> x1, Pallas kernels: none -> 139 us  [fused(): pl.pallas_call(functools.partial(kernel, n), out_shape=(jax.ShapeDtypeStr...]
    reduce_sum x16 -> x0, other arithmetic: 80 us -> none  [the longest x8 40.9 us: col_part(): return (running + jnp.sum(ratios, axis=0), None)]
    all_gather x2 -> x0, waiting for transfers between devices: 75.3 us -> none  [on_device(): every_row = lax.all_gather(levels, 'src', axis=0, tiled=True)]
    dot_general x2 -> x0, matrix products: 70 us -> none  [on_device(): jnp.dot(coefficients, columns, preferred_element_type=jnp.float32, precis...]
    another operation x5 -> x0, loops' own time: 52.4 us -> none  [the longest x2 21.1 us: on_device(): lax.scan(col_part, jnp.zeros((cols_dev,), jnp.float32), offsets)]
    dynamic_update_slice x4 -> x0, other arithmetic: 25 us -> none  [on_device(): coefficients = lax.map(coeff_block, offsets).reshape(rows_dev, cols_dev)]
    dynamic_slice x84 -> x0, local copies, waits for them, and re-layouts: 16.5 us -> none  [the longest x20 11.7 us: on_device(): row_partial = lax.map(row_part, offsets).reshape(rows_dev)]
  transfers between devices with their start and end apart: 4 -> 0, of which waited for: 4 -> 0; matrix products, arithmetic and copies ran while one was open for 5% -> 0% of each run, Pallas kernels for 0% -> 0%
where the time goes in v1:
time: 152 us
  Pallas kernels  139 us (91%)
  local copies, waits for them, and re-layouts  9.85 us (6%)
  other arithmetic  1.61 us (1%)
    pallas_call x1, Pallas kernels, fused(): pl.pallas_call(functools.partial(kernel, n), out_shape=(jax.ShapeDtypeStr...  139 us
    another operation x21, local copies, waits for them, and re-layouts, features(): jnp.stack(head + tail + (zero,) * 8, axis=1 if left else 0)  3.34 us
    unnamed x16, local copies, waits for them, and re-layouts  3.24 us

profile of v1, /device:TPU:0, one launch (start us, length us, event | category | flops | bytes accessed | tf_op | source)
XLA Modules:
  0.0 151.7 jit_solution(14434097172528965397)
XLA Ops:
  0.6 0.8 and_convert_fusion.2
  1.6 0.0 copy-start.1
  1.6 0.7 copy.21.left_ref
  2.3 0.1 copy-done.1
  2.4 0.1 and_convert_fusion
  2.9 0.0 copy-start.4
  2.9 2.2 %stack.83.right_ref = bf16[16,16384]{1,0:T(8,128)(2,1)} concatenate(bf16[1,16384]{1,0:T(2,128)(2,1)S(1)} %stack.75, bf16[1,16384]{1,0:T(2,128)(2,1)S(1)} %stack.76, bf16[1,16384]{1,0:T(2,128)(2,1)S(1)} %stack.77, bf16[1,16384]{1,0:T(2,128)(2,1)S(1)} %stack.78, bf16[1,16384]{1,0:T(2,128)(2,1)S(1)} %stack_broadcast_in_dim.7, bf16[1,16384]{1,0:T(2,128)(2,1)S(1)} %stack.79, ...), dimensions={0} | concatenate | bytes 1048576 | tf_op jit(solution)/shard_map/stack | solution.py:266
  5.1 0.0 copy-done.4
  5.1 0.0 copy-start.5
  5.1 0.9 copy.22.od_ref
  6.0 0.0 copy-done.5
  6.0 0.0 copy-start.3
  6.0 0.8 copy.23.ret_ref
  6.8 0.0 copy-done.3
  6.8 0.9 copy.24.dem_ref
  7.7 0.0 copy-start.6
  7.7 0.7 copy-done.6
  8.4 0.7 copy.25.scen_ref
  9.1 139.4 %shard_map.85 = (f32[512,1]{1,0:T(8,128)}, f32[32,1,512]{2,1,0:T(1,128)}, f32[512,32]{1,0:T(8,128)}) custom-call(bf16[512,16]{1,0:T(8,128)(2,1)} %copy.21.left_ref, bf16[16,16384]{1,0:T(8,128)(2,1)} %stack.83.right_ref, f32[512,1]{1,0:T(8,128)} %copy.22.od_ref, f32[512,1]{1,0:T(8,128)} %copy.23.ret_ref, f32[512,1]{1,0:T(8,128)} %copy.24.dem_ref, ...), custom_call_target="tpu_custom_call" | custom-call | tf_op jit(solution)/shard_map/pallas_call | solution.py:270
  148.5 0.0 copy-start
  148.5 1.7 %copy.26 = f32[512,32]{0,1:T(8,128)} copy(f32[512,32]{1,0:T(8,128)} %get-tuple-element.17) | data formatting | bytes 131072
  150.2 0.0 copy-done
  150.2 0.0 copy-start.2
  150.2 0.7 reduce
  150.9 0.1 copy-done.2
  151.1 0.6 copy.28
  (21 shorter events, 0.4 us)
Async XLA Ops:
  1.6 0.8 copy-start.1
  2.9 2.2 %copy-start.4 = (f32[512]{0:T(512)S(1)}, f32[512]{0:T(512)}, u32[]{:S(2)}) copy-start(f32[512]{0:T(512)} %param.6) | copy-start | bytes 6148
  5.1 0.9 copy-start.5
  6.0 0.9 copy-start.3
  7.7 0.7 copy-start.6
  148.5 1.7 %copy-start = (f32[512,1]{1,0:T(8,128)S(1)}, f32[512,1]{1,0:T(8,128)}, u32[]{:S(2)}) copy-start(f32[512,1]{1,0:T(8,128)} %get-tuple-element.6) | copy-start | bytes 6148
  150.2 0.8 copy-start.2

commit v2 on v1

--- a/solution.py
+++ b/solution.py
@@ -56,6 +56,19 @@
     firms = rows * n
     scen = scen_ref.shape[0]
     wide = rows // LANES
+    chips = n // 2
+    planes = n // 8
+    plane = lax.div(me, 8)
+    chip_xy = lax.div(lax.rem(me, 8), 2)
+    core = lax.rem(me, 2)
+
+    def slot_of(d):
+        return lax.rem(d, 2) * chips + lax.div(d, 2)
+
+    def firm_block(p):
+        return lax.rem(p, chips) * 2 + lax.div(p, chips)
+
+    here = slot_of(me)
 
     barrier = pltpu.get_barrier_semaphore()
 
@@ -70,8 +83,8 @@
         def _(s):
             q = lax.rem(me + n - s, n)
             pltpu.make_async_remote_copy(
-                src_ref=src(q),
-                dst_ref=dst.at[me],
+                src_ref=src(slot_of(q)),
+                dst_ref=dst.at[here],
                 send_sem=send_sem.at[phase],
                 recv_sem=sems,
                 device_id={"src": q},
@@ -81,7 +94,7 @@
         some = buf.at[pl.ds(0, n - 1)]
         pltpu.make_async_copy(some, some, sem).wait()
 
-    dem_all[me] = dem_row_ref[...]
+    dem_all[here] = dem_row_ref[...]
     push(lambda q: dem_row_ref, dem_all, one_sem.at[0], 0)
 
     @pl.loop(0, n)
@@ -89,30 +102,34 @@
         c0 = pl.multiple_of(q * rows, rows)
         dist = jnp.dot(
             left_ref[...],
-            right_ref[:, pl.ds(c0, rows)],
+            right_ref[:, pl.ds(pl.multiple_of(firm_block(q) * rows, rows), rows)],
             preferred_element_type=jnp.float32,
         )
         bmat[:, pl.ds(c0, rows)] = jnp.where(dist <= RANGE * RANGE, 1.0, FAR)
 
-    mine = pl.ds(pl.multiple_of(me * rows, rows), rows)
+    mine = pl.ds(pl.multiple_of(here * rows, rows), rows)
     for r0 in range(0, rows, ROWS):
         shape = (ROWS, rows)
         same = lax.broadcasted_iota(jnp.int32, shape, 0) + r0 == lax.broadcasted_iota(
             jnp.int32, shape, 1
         )
-        bmat[pl.ds(r0, ROWS), mine] = jnp.where(same, jnp.inf, bmat[pl.ds(r0, ROWS), mine])
+        bmat[pl.ds(r0, ROWS), mine] = jnp.where(same, FAR * FAR * 1e12, bmat[pl.ds(r0, ROWS), mine])
 
     xb[...] = jnp.broadcast_to(jnp.sqrt(od_ref[...]), xb.shape)
 
     @pl.loop(0, n)
     def _(q):
         c0 = pl.multiple_of(q * rows, rows)
-        y = jnp.sqrt(ind_ref[q])
+        y = jnp.sqrt(ind_ref[firm_block(q)])
         yrow[:, pl.ds(c0, rows)] = y
         urow[:, pl.ds(c0, rows)] = 1.0 / y
 
-    tiles = 16
+    tiles = 32
     strip = tiles * LANES
+
+    def pair_sum(a, b):
+        return (a + b) * pltpu.reciprocal(a * b, approx=True)
+
     for sweep in range(SWEEPS):
         @pl.loop(0, rows // ROWS)
         def _(b):
@@ -121,9 +138,12 @@
 
             def body(c, total):
                 c0 = pl.multiple_of(c * strip, strip)
-                for t in range(tiles):
-                    cs = pl.ds(c0 + t * LANES, LANES)
-                    total = total + pl.reciprocal(bmat[rs, cs] * urow[:, cs] + x, approx=True)
+                for t in range(0, tiles, 2):
+                    ca = pl.ds(c0 + t * LANES, LANES)
+                    cb = pl.ds(c0 + (t + 1) * LANES, LANES)
+                    total = total + pair_sum(
+                        bmat[rs, ca] * urow[:, ca] + x, bmat[rs, cb] * urow[:, cb] + x
+                    )
                 return total
 
             rowacc[rs, :] = lax.fori_loop(
@@ -142,19 +162,20 @@
                 cs = pl.ds(c0 + t * LANES, LANES)
                 y = yrow[:, cs]
                 total = jnp.zeros((8, LANES), jnp.float32)
-                for r0 in range(0, rows, ROWS):
+                for r0 in range(0, rows, 2 * ROWS):
                     rs = pl.ds(r0, ROWS)
-                    term = pl.reciprocal(bmat[rs, cs] * vb[rs, :] + y, approx=True)
+                    rt = pl.ds(r0 + ROWS, ROWS)
+                    term = pair_sum(bmat[rs, cs] * vb[rs, :] + y, bmat[rt, cs] * vb[rt, :] + y)
                     total = total + jnp.sum(term.reshape(ROWS // 8, 8, LANES), axis=0)
                 part[sweep, q, :, pl.ds(t * LANES, LANES)] = jnp.sum(total, axis=0, keepdims=True)
 
-        gath[2 * sweep, me] = part[sweep, me]
+        gath[2 * sweep, here] = part[sweep, here]
         push(lambda q: part.at[sweep, q], gath.at[2 * sweep], one_sem.at[1 + 2 * sweep], 1 + 2 * sweep)
         drain(gath.at[2 * sweep], one_sem.at[1 + 2 * sweep])
         col_total = jnp.sum(gath[2 * sweep], axis=0)
         fresh = gath.at[2 * sweep + 1]
-        fresh[me] = firms * ind_ref[me] / col_total
-        push(lambda q: fresh.at[me], fresh, one_sem.at[2 + 2 * sweep], 2 + 2 * sweep)
+        fresh[here] = firms * ind_ref[me] / col_total
+        push(lambda q: fresh.at[here], fresh, one_sem.at[2 + 2 * sweep], 2 + 2 * sweep)
         drain(fresh, one_sem.at[2 + 2 * sweep])
 
         @pl.loop(0, n)
@@ -164,8 +185,17 @@
             yrow[:, pl.ds(c0, rows)] = y
             urow[:, pl.ds(c0, rows)] = 1.0 / y
 
-    y_out[...] = gath[2 * SWEEPS - 1]
+    @pl.loop(0, n)
+    def _(q):
+        y_out[firm_block(q)] = gath[2 * SWEEPS - 1, q]
+
     x_new = xb[:, 0:1]
+    for r0 in range(0, rows, ROWS):
+        shape = (ROWS, rows)
+        same = lax.broadcasted_iota(jnp.int32, shape, 0) + r0 == lax.broadcasted_iota(
+            jnp.int32, shape, 1
+        )
+        bmat[pl.ds(r0, ROWS), mine] = jnp.where(same, jnp.inf, bmat[pl.ds(r0, ROWS), mine])
     x_out[...] = x_new
     gain = x_new * (ret_ref[...] / (firms * od_ref[...]))
     drain(dem_all, one_sem.at[0])
@@ -183,60 +213,91 @@
             hi_ref[...], both, dims, preferred_element_type=jnp.float32
         ) + lax.dot_general(lo_ref[...], both, dims, preferred_element_type=jnp.float32)
 
-    def split(rs, value):
+    def split(rs, cs, value):
         top = value.astype(jnp.bfloat16)
-        hi_ref[rs, :] = top
-        lo_ref[rs, :] = (value - top.astype(jnp.float32)).astype(jnp.bfloat16)
+        hi_ref[rs, cs] = top
+        lo_ref[rs, cs] = (value - top.astype(jnp.float32)).astype(jnp.bfloat16)
 
     acc[...] = jnp.zeros_like(acc)
 
-    @pl.loop(0, n)
-    def _(q):
-        cs = pl.ds(pl.multiple_of(q * rows, rows), rows)
-        u = urow[:, cs]
+    @pl.loop(0, n // 4)
+    def _(g):
+        for k in range(4):
+            at = pl.ds(pl.multiple_of((4 * g + k) * rows, rows), rows)
+            u = urow[:, at]
+            for r0 in range(0, rows, ROWS):
+                rs = pl.ds(r0, ROWS)
+                x = jnp.concatenate([xb[rs, :]] * wide, axis=1)
+                value = pltpu.reciprocal(bmat[rs, at] * u + x, approx=True)
+                bmat[rs, at] = value
+                split(rs, pl.ds(k * rows, rows), value)
+        blocks = [4 * g + k for k in range(4)]
+        product(
+            jnp.concatenate(
+                [jnp.where(kept(firm_block(p)), dem_all[p], 0.0) for p in blocks], axis=1
+            )
+        )
+
+    summed = gain * (acc[:, 0:scen] + acc[:, scen:])
+    keep_mine = kept(me)
+    lev_all[here] = jnp.where(keep_mine, dem_row_ref[...] + summed.T, 0.0)
+    acc[...] = jnp.zeros_like(acc)
+
+    def send(ref, sem, target):
+        pltpu.make_async_remote_copy(
+            src_ref=ref,
+            dst_ref=ref,
+            send_sem=send_sem.at[5],
+            recv_sem=sem,
+            device_id={"src": target},
+        ).start()
+
+    def wait(count, sem):
+        some = lev_all.at[pl.ds(0, count)]
+        pltpu.make_async_copy(some, some, sem).wait()
+
+    def slots(c, k):
+        return c * chips + lax.rem(plane + k, planes) * 4
+
+    def to_plane(k):
+        block = lev_all.at[pl.ds(slots(core, k) + chip_xy, 1)]
+        for s in range(1, 4):
+            send(block, lev_sem.at[k], plane * 8 + lax.rem(chip_xy + s, 4) * 2 + core)
+
+    def to_core(k):
+        send(lev_all.at[pl.ds(slots(core, k), 4)], lev_sem.at[2 * planes + k], me + 1 - 2 * core)
+
+    def multiply(c, k):
+        first = slots(c, k)
         for r0 in range(0, rows, ROWS):
             rs = pl.ds(r0, ROWS)
-            x = jnp.concatenate([xb[rs, :]] * wide, axis=1)
-            value = pl.reciprocal(bmat[rs, cs] * u + x, approx=True)
-            bmat[rs, cs] = value
-            split(rs, value)
-        product(jnp.where(kept(q), dem_all[q], 0.0))
+            for j in range(4):
+                at = pl.ds(pl.multiple_of((first + j) * rows, rows), rows)
+                split(rs, pl.ds(j * rows, rows), bmat[rs, at])
+        product(jnp.concatenate([lev_all[first + j] for j in range(4)], axis=1))
+
+    own = lev_all.at[pl.ds(here, 1)]
+    for k in range(1, planes):
+        target = lax.rem(plane + planes - k, planes) * 8 + lax.rem(me, 8)
+        send(own, lev_sem.at[planes + k], target)
+    to_plane(0)
+    wait(3, lev_sem.at[0])
+    to_core(0)
+    for k in range(1, planes):
+        wait(1, lev_sem.at[planes + k])
+        to_plane(k)
+        if k == 1:
+            multiply(core, 0)
+    wait(4, lev_sem.at[2 * planes])
+    multiply(1 - core, 0)
+    for k in range(1, planes):
+        wait(3, lev_sem.at[k])
+        to_core(k)
+        multiply(core, k)
+        wait(4, lev_sem.at[2 * planes + k])
+        multiply(1 - core, k)
 
     summed = gain * (acc[:, 0:scen] + acc[:, scen:])
-    keep_mine = kept(me)
-    fresh_levels = jnp.where(keep_mine, dem_row_ref[...] + summed.T, 0.0)
-    lev_all[me] = fresh_levels
-    acc[...] = jnp.zeros_like(acc)
-    lev_mine = lev_all.at[me]
-
-    @pl.loop(1, n)
-    def _(s):
-        q = lax.rem(me + n - s, n)
-        pltpu.make_async_remote_copy(
-            src_ref=lev_mine,
-            dst_ref=lev_all.at[me],
-            send_sem=send_sem.at[5],
-            recv_sem=lev_sem.at[me],
-            device_id={"src": q},
-        ).start()
-
-    @pl.loop(0, n)
-    def _(s):
-        q = lax.rem(me + s, n)
-        cs = pl.ds(pl.multiple_of(q * rows, rows), rows)
-        for r0 in range(0, rows, ROWS):
-            rs = pl.ds(r0, ROWS)
-            split(rs, bmat[rs, cs])
-
-        @pl.when(s > 0)
-        def _():
-            slot = lev_all.at[q]
-            pltpu.make_async_copy(slot, slot, lev_sem.at[q]).wait()
-
-        product(lev_all[q])
-
-    summed = gain * (acc[:, 0:scen] + acc[:, scen:])
-    ids = me * rows + lax.broadcasted_iota(jnp.int32, (scen, rows), 1)
     lev_out[...] = jnp.where(keep_mine, dem_row_ref[...] + summed.T, 0.0).T
 
     drain(dem_all, send_sem.at[0])
@@ -278,8 +339,8 @@
         out_specs=(vmem,) * 3,
         scratch_shapes=[
             pltpu.VMEM((rows, cols), f32),
-            pltpu.VMEM((rows, rows), jnp.bfloat16),
-            pltpu.VMEM((rows, rows), jnp.bfloat16),
+            pltpu.VMEM((rows, 4 * rows), jnp.bfloat16),
+            pltpu.VMEM((rows, 4 * rows), jnp.bfloat16),
             pltpu.VMEM((rows, LANES), f32),
             pltpu.VMEM((rows, LANES), f32),
             pltpu.VMEM((rows, LANES), f32),
@@ -292,7 +353,7 @@
             pltpu.VMEM((rows, 2 * scen), f32),
             pltpu.SemaphoreType.DMA((6,)),
             pltpu.SemaphoreType.DMA((5,)),
-            pltpu.SemaphoreType.DMA((n,)),
+            pltpu.SemaphoreType.DMA((3 * n // 8,)),
         ],
         compiler_params=pltpu.CompilerParams(
             collective_id=0, has_side_effects=True, vmem_limit_bytes=56 * 2**20
@@ -396,7 +457,7 @@
     rows = out_density.shape[0]
     cols = in_density.shape[0]
     whole = lax.axis_size("dst") == 1
-    if whole and rows % (2 * LANES) == 0 and cols % (16 * LANES) == 0:
+    if whole and rows % (2 * LANES) == 0 and cols % (32 * LANES) == 0 and lax.axis_size("src") % 8 == 0:
         return fused(*args)
     return on_device(*args)
 

time: 152 us -> 109 us (0.72)
  Pallas kernels: 139 us -> 96.2 us
    pallas_call x1, Pallas kernels: 139 us -> 96.2 us  [fused(): pl.pallas_call(functools.partial(kernel, n), out_shape=(jax.ShapeDtypeStr...]
where the time goes in v2:
time: 109 us; the launch traced here: 108 us
  Pallas kernels  96.2 us (88%)
  local copies, waits for them, and re-layouts  9.85 us (9%)
  other arithmetic  1.61 us (1%)
    pallas_call x1, Pallas kernels, fused(): pl.pallas_call(functools.partial(kernel, n), out_shape=(jax.ShapeDtypeStr...  96.2 us
    another operation x21, local copies, waits for them, and re-layouts, features(): jnp.stack(head + tail + (zero,) * 8, axis=1 if left else 0)  3.34 us
    unnamed x16, local copies, waits for them, and re-layouts  3.24 us

profile of v2, /device:TPU:0, one launch (start us, length us, event | category | flops | bytes accessed | tf_op | source)
XLA Modules:
  0.0 108.5 jit_solution(8710199163010609911)
XLA Ops:
  0.6 0.8 and_convert_fusion.2
  1.6 0.0 copy-start.1
  1.6 0.7 copy.21.left_ref
  2.3 0.1 copy-done.1
  2.4 0.1 and_convert_fusion
  2.9 0.0 copy-start.4
  2.9 2.2 %stack.83.right_ref = bf16[16,16384]{1,0:T(8,128)(2,1)} concatenate(bf16[1,16384]{1,0:T(2,128)(2,1)S(1)} %stack.75, bf16[1,16384]{1,0:T(2,128)(2,1)S(1)} %stack.76, bf16[1,16384]{1,0:T(2,128)(2,1)S(1)} %stack.77, bf16[1,16384]{1,0:T(2,128)(2,1)S(1)} %stack.78, bf16[1,16384]{1,0:T(2,128)(2,1)S(1)} %stack_broadcast_in_dim.7, bf16[1,16384]{1,0:T(2,128)(2,1)S(1)} %stack.79, ...), dimensions={0} | concatenate | bytes 1048576 | tf_op jit(solution)/shard_map/stack | solution.py:327
  5.1 0.0 copy-done.4
  5.1 0.0 copy-start.5
  5.1 0.9 copy.22.od_ref
  6.0 0.0 copy-done.5
  6.0 0.0 copy-start.3
  6.0 0.8 copy.23.ret_ref
  6.8 0.0 copy-done.3
  6.8 0.9 copy.24.dem_ref
  7.7 0.0 copy-start.6
  7.7 0.7 copy-done.6
  8.4 0.7 copy.25.scen_ref
  9.1 96.2 %shard_map.85 = (f32[512,1]{1,0:T(8,128)}, f32[32,1,512]{2,1,0:T(1,128)}, f32[512,32]{1,0:T(8,128)}) custom-call(bf16[512,16]{1,0:T(8,128)(2,1)} %copy.21.left_ref, bf16[16,16384]{1,0:T(8,128)(2,1)} %stack.83.right_ref, f32[512,1]{1,0:T(8,128)} %copy.22.od_ref, f32[512,1]{1,0:T(8,128)} %copy.23.ret_ref, f32[512,1]{1,0:T(8,128)} %copy.24.dem_ref, ...), custom_call_target="tpu_custom_call" | custom-call | tf_op jit(solution)/shard_map/pallas_call | solution.py:331
  105.3 0.0 copy-start
  105.3 1.7 %copy.26 = f32[512,32]{0,1:T(8,128)} copy(f32[512,32]{1,0:T(8,128)} %get-tuple-element.17) | data formatting | bytes 131072
  107.0 0.0 copy-done
  107.0 0.0 copy-start.2
  107.0 0.7 reduce
  107.7 0.1 copy-done.2
  107.8 0.6 copy.28
  (21 shorter events, 0.4 us)
Async XLA Ops:
  1.6 0.8 copy-start.1
  2.9 2.2 %copy-start.4 = (f32[512]{0:T(512)S(1)}, f32[512]{0:T(512)}, u32[]{:S(2)}) copy-start(f32[512]{0:T(512)} %param.6) | copy-start | bytes 6148
  5.1 0.9 copy-start.5
  6.0 0.9 copy-start.3
  7.7 0.7 copy-start.6
  105.3 1.7 %copy-start = (f32[512,1]{1,0:T(8,128)S(1)}, f32[512,1]{1,0:T(8,128)}, u32[]{:S(2)}) copy-start(f32[512,1]{1,0:T(8,128)} %get-tuple-element.6) | copy-start | bytes 6148
  107.0 0.8 copy-start.2
